TPU v7x, 32 devices: a whole 2x2x4 slice. The times are simulated.
32 devices in a mesh: sample: 2 (over x), ctx: 16 (over z, y, core).
Axes of the slice: x: 2, y: 2, z: 4, core: 2. Of those that a mesh axis runs over, the one named last changes fastest.
Arguments:
- queries: bfloat16 [4, 512, 8192], P('sample', None, 'ctx'), may hold values from -8 to 8
- prompt_key_value: bfloat16 [2, 512, 1024], P(None, 'ctx', 'sample'), may hold values from -6 to 6
- continuation_key_value: bfloat16 [2, 4, 512, 1024], P(None, 'sample', 'ctx'), may hold values from -6 to 6
- page_owner: int32 [512], replicated, may hold values from 0 to 4, as said below
- cont_lengths: int32 [4], replicated, may hold values from 2 to 512, as said below
- branch_offsets: int32 [4], replicated, may hold values from 128 to 512
Outputs:
- attended: bfloat16 [4, 512, 8192], P('sample', None, 'ctx')
Inputs may be any that keep to these rules, and one draw needn't show every extreme that they name: `page_owner`: constant over each aligned page of 16 positions; 0 marks a page seen by every continuation that branches after it, s + 1 a page seen only by continuation s; some page belongs to continuation 4 - 1. `cont_lengths`: some continuation has all 512 positions live.
All inputs are finite; a program needn't handle non-finite values.
Results may differ from a plain program's by a relative error of at most 0.0045.
Values may be sent and summed in bfloat16 or wider, within the bound.
A program may use at most 64 MiB of HBM per device.

v0:
```python
import functools
import math

import jax
import jax.numpy as jnp
from jax import lax
from jax.experimental import pallas as pl
from jax.experimental.pallas import tpu as pltpu
from jax.sharding import PartitionSpec as P

KEY_VALUE_HEADS = 8
HEAD_SIZE = 128
MESH = pl.DeviceIdType.MESH

neg_large = -1e30
query_block = 128


def gather_kernel(
    samples,
    ctx,
    prompt_ref,
    cont_ref,
    own_prompt,
    own_cont,
    swapped,
    swap_sems,
    cross_sems,
    relay_send,
    relay_recv,
    prompt_send,
    prompt_recv,
    cont_send,
    cont_forward,
    cont_recv,
):
    groups = KEY_VALUE_HEADS
    copies = ctx // groups
    shard_heads = prompt_ref.shape[2] // HEAD_SIZE
    sample = lax.axis_index("sample")
    me = lax.axis_index("ctx")
    group = me // copies
    rank = lax.rem(me, copies)

    siblings = [group * copies + lax.rem(rank + k, copies) for k in range(1, copies)]

    barrier = pltpu.get_barrier_semaphore()
    count = 0
    for ds in range(samples):
        for j in range(groups):
            if ds == 0 and j == 0:
                continue
            peer = lax.rem(group + j, groups) * copies + rank
            pl.semaphore_signal(
                barrier,
                inc=1,
                device_id=(lax.rem(sample + ds, samples), peer),
                device_id_type=MESH,
            )
            count += 1
    for sibling in siblings:
        pl.semaphore_signal(
            barrier, inc=1, device_id=(sample, sibling), device_id_type=MESH
        )
        count += 1
    pl.semaphore_wait(barrier, count)

    def head_columns(head):
        return pl.ds(pl.multiple_of(head * HEAD_SIZE, HEAD_SIZE), HEAD_SIZE)

    sends = []

    def send(src, dst, send_sem, recv_sem, device_id):
        copy = pltpu.make_async_remote_copy(
            src_ref=src,
            dst_ref=dst,
            send_sem=send_sem,
            recv_sem=recv_sem,
            device_id=device_id,
            device_id_type=MESH,
        )
        copy.start()
        return copy

    own_piece = cont_ref.at[:, :, :, head_columns(group)]
    pltpu.make_async_copy(own_piece, own_cont.at[:, :, group, rank], cont_recv.at[me]).start()

    def wait_slot(buffer, sem):
        pltpu.make_async_copy(buffer, buffer, sem).wait()

    def start_unless(mine, copy, src, dst, recv_sem):
        @pl.when(mine)
        def _():
            pltpu.make_async_copy(src, dst, recv_sem).start()

        @pl.when(jnp.logical_not(mine))
        def _():
            copy.start()

        sends.append((copy, jnp.logical_not(mine)))

    def send_cont(j):
        target = lax.rem(group + j, groups)
        sends.append(
            send(
                cont_ref.at[:, :, :, head_columns(target)],
                own_cont.at[:, :, group, rank],
                cont_send.at[j],
                cont_recv.at[me],
                (sample, target * copies + rank),
            )
        )

    def send_prompt(kind, part, ds, source, shard):
        local = lax.rem(part + group, shard_heads)
        head = shard * shard_heads + local
        target_sample = lax.rem(sample + ds, samples)
        index = part * samples + ds + (shard_heads * samples if kind == 1 else 0)
        if kind is None:
            src = source.at[:, :, head_columns(local)]
            dst = own_prompt.at[:, group, rank]
        else:
            src = source.at[:, head_columns(local)]
            dst = own_prompt.at[kind, group, rank]
        copy = pltpu.make_async_remote_copy(
            src_ref=src,
            dst_ref=dst,
            send_sem=prompt_send.at[index],
            recv_sem=prompt_recv.at[group],
            device_id=(target_sample, head * copies + rank),
            device_id_type=MESH,
        )
        if ds == 0:
            start_unless(head == group, copy, src, dst, prompt_recv.at[group])
        else:
            copy.start()
            sends.append(copy)

    def relay(buffer, index):
        for k, sibling in enumerate(siblings):
            sends.append(
                send(
                    buffer,
                    buffer,
                    relay_send.at[index, k],
                    relay_recv.at[index, rank],
                    (sample, sibling),
                )
            )

    half = groups // 2
    order = sorted(range(1, groups), key=lambda j: (abs(j - half), j))
    early, late = order[: half - 1], order[half - 1 :]
    if samples == 2:
        other = 1 - sample
        swap = send(prompt_ref.at[1], swapped, swap_sems.at[0], swap_sems.at[1], (other, me))
        for part in range(shard_heads):
            send_prompt(0, part, 0, prompt_ref.at[0], sample)
        for j in early:
            send_cont(j)
        swap.wait_recv()
        for part in range(shard_heads):
            send_prompt(1, part, 0, swapped, other)
        for j in late:
            send_cont(j)
    else:
        for part in range(shard_heads):
            for ds in range(samples):
                send_prompt(None, part, ds, prompt_ref, sample)
        for j in order:
            send_cont(j)

    for k, sibling in enumerate(siblings):
        sends.append(
            send(
                own_piece,
                own_cont.at[:, :, group, rank],
                cont_forward.at[0, k],
                cont_recv.at[me],
                (sample, sibling),
            )
        )
    wait_slot(own_cont.at[:, :, group, rank], cont_recv.at[me])

    def forward_cont(j):
        source = lax.rem(group + groups - j, groups)
        slot = source * copies + rank
        wait_slot(own_cont.at[:, :, source, rank], cont_recv.at[slot])
        for k, sibling in enumerate(siblings):
            sends.append(
                send(
                    own_cont.at[:, :, source, rank],
                    own_cont.at[:, :, source, rank],
                    cont_forward.at[j, k],
                    cont_recv.at[slot],
                    (sample, sibling),
                )
            )

    if samples == 2:
        direct = lax.rem(group // shard_heads + sample, 2)
        arrived = own_prompt.at[direct, :, rank]
        crossed = own_prompt.at[1 - direct, :, rank]
        for j in range(groups):
            wait_slot(own_prompt.at[direct, j, rank], prompt_recv.at[j])
        sends.append(send(arrived, arrived, cross_sems.at[0], cross_sems.at[1], (other, me)))
        relay(arrived, 0)
        for j in early:
            forward_cont(j)
        wait_slot(crossed, cross_sems.at[1])
        relay(crossed, 1)
        for j in late:
            forward_cont(j)
        swap.wait_send()
    else:
        for j in range(groups):
            wait_slot(own_prompt.at[:, j, rank], prompt_recv.at[j])
        relay(own_prompt.at[:, :, rank], 0)
        for j in order:
            forward_cont(j)

    for k in range(1, copies):
        peer = lax.rem(rank + copies - k, copies)
        if samples == 2:
            wait_slot(own_prompt.at[direct, :, peer], relay_recv.at[0, peer])
            wait_slot(own_prompt.at[1 - direct, :, peer], relay_recv.at[1, peer])
        else:
            wait_slot(own_prompt.at[:, :, peer], relay_recv.at[0, peer])
        for j in range(groups):
            wait_slot(own_cont.at[:, :, j, peer], cont_recv.at[j * copies + peer])

    for item in sends:
        if isinstance(item, tuple):
            copy, started = item

            @pl.when(started)
            def _():
                copy.wait_send()
        else:
            item.wait_send()


def gather(prompt, cont, samples, ctx):
    groups = KEY_VALUE_HEADS
    copies = ctx // groups
    prompt_rows = prompt.shape[1]
    here, cont_rows = cont.shape[1:3]
    shard_heads = prompt.shape[2] // HEAD_SIZE
    forwards = max(copies - 1, 1)
    anywhere = pl.BlockSpec(memory_space=pl.ANY)
    own_prompt, own_cont = pl.pallas_call(
        functools.partial(gather_kernel, samples, ctx),
        out_shape=(
            jax.ShapeDtypeStruct((2, groups, copies, prompt_rows, HEAD_SIZE), prompt.dtype),
            jax.ShapeDtypeStruct((2, here, groups, copies, cont_rows, HEAD_SIZE), cont.dtype),
        ),
        in_specs=[anywhere, anywhere],
        out_specs=(anywhere, anywhere),
        scratch_shapes=[
            pltpu.VMEM(prompt.shape[1:], prompt.dtype),
            pltpu.SemaphoreType.DMA((2,)),
            pltpu.SemaphoreType.DMA((2,)),
            pltpu.SemaphoreType.DMA((2, forwards)),
            pltpu.SemaphoreType.DMA((2, copies)),
            pltpu.SemaphoreType.DMA((2 * shard_heads * samples,)),
            pltpu.SemaphoreType.DMA((groups,)),
            pltpu.SemaphoreType.DMA((groups,)),
            pltpu.SemaphoreType.DMA((groups, forwards)),
            pltpu.SemaphoreType.DMA((ctx,)),
        ],
        compiler_params=pltpu.CompilerParams(collective_id=0, has_side_effects=True),
        name="gather_heads",
    )(prompt, cont)
    own_prompt = own_prompt.reshape(2, ctx * prompt_rows, HEAD_SIZE)
    own_cont = own_cont.reshape(2, here, ctx * cont_rows, HEAD_SIZE)
    return own_prompt, own_cont


def attend_kernel(block, lengths, offsets, base, owner_ref, q_ref, prompt_ref, cont_ref, out_ref):
    heads = q_ref.shape[2] // HEAD_SIZE
    prompt_len = prompt_ref.shape[1]
    blocks = cont_ref.shape[2] // block
    sample = base[0] + pl.program_id(0)
    step = pl.program_id(1)
    length = lengths[sample]
    factor = HEAD_SIZE ** -0.5 * math.log2(math.e)
    contract_last = (((1,), (1,)), ((), ()))

    live = step * block < length

    @pl.when(jnp.logical_not(live))
    def _():
        out_ref[...] = jnp.zeros_like(out_ref)

    def with_ones(values):
        return jnp.concatenate([values, jnp.ones_like(values)], axis=1)

    for i in range(blocks):

        @pl.when(live & (step == i))
        def _():
            extent = (i + 1) * block
            q = jnp.concatenate(
                [q_ref[0, :, h * HEAD_SIZE : (h + 1) * HEAD_SIZE] for h in range(heads)], axis=0
            )
            owner = owner_ref[...]
            position = lax.broadcasted_iota(jnp.int32, (1, prompt_len), 1)
            seen = ((owner == 0) | (owner == sample + 1)) & (position < offsets[sample])
            bias = jnp.where(seen, 0.0, neg_large)
            first = lax.dot_general(
                q, prompt_ref[0], contract_last, preferred_element_type=jnp.float32
            )
            first = first + bias
            second = lax.dot_general(
                q, cont_ref[0, 0, :extent], contract_last, preferred_element_type=jnp.float32
            )
            row = lax.broadcasted_iota(jnp.int32, (block, block), 0)
            col = lax.broadcasted_iota(jnp.int32, (block, block), 1)
            causal = jnp.where(col <= row, 0.0, neg_large)
            causal = jnp.concatenate([causal] * heads, axis=0)
            diagonal = second[:, i * block :] + causal
            if i:
                second = jnp.concatenate([second[:, : i * block], diagonal], axis=1)
            else:
                second = diagonal
            row_max = jnp.maximum(
                jnp.max(first, axis=1, keepdims=True), jnp.max(second, axis=1, keepdims=True)
            )
            first = jnp.exp2((first - row_max) * factor).astype(jnp.bfloat16)
            second = jnp.exp2((second - row_max) * factor).astype(jnp.bfloat16)
            total = jnp.dot(
                first, with_ones(prompt_ref[1]), preferred_element_type=jnp.float32
            ) + jnp.dot(
                second, with_ones(cont_ref[1, 0, :extent]), preferred_element_type=jnp.float32
            )
            mixed = total[:, :HEAD_SIZE] / total[:, HEAD_SIZE:]
            place = i * block + lax.broadcasted_iota(jnp.int32, (block, HEAD_SIZE), 0)
            for h in range(heads):
                out_ref[0, :, h * HEAD_SIZE : (h + 1) * HEAD_SIZE] = jnp.where(
                    place < length, mixed[h * block : (h + 1) * block], 0.0
                ).astype(out_ref.dtype)


def attend(queries, own_prompt, own_cont, page_owner, lengths, offsets, base):
    here, cont_len, width = queries.shape
    prompt_len = own_prompt.shape[1]
    block = math.gcd(query_block, cont_len)
    return pl.pallas_call(
        functools.partial(attend_kernel, block),
        out_shape=jax.ShapeDtypeStruct(queries.shape, queries.dtype),
        grid_spec=pltpu.PrefetchScalarGridSpec(
            num_scalar_prefetch=3,
            grid=(here, cont_len // block),
            in_specs=[
                pl.BlockSpec((1, prompt_len), lambda s, i, *_: (0, 0)),
                pl.BlockSpec((1, block, width), lambda s, i, *_: (s, i, 0)),
                pl.BlockSpec((2, prompt_len, HEAD_SIZE), lambda s, i, *_: (0, 0, 0)),
                pl.BlockSpec((2, 1, cont_len, HEAD_SIZE), lambda s, i, *_: (0, s, 0, 0)),
            ],
            out_specs=pl.BlockSpec((1, block, width), lambda s, i, *_: (s, i, 0)),
        ),
        compiler_params=pltpu.CompilerParams(vmem_limit_bytes=60 * 1024 * 1024),
        name="attend",
    )(lengths, offsets, base, page_owner[None, :], queries, own_prompt, own_cont)


def solution(mesh):
    samples, ctx = mesh.shape["sample"], mesh.shape["ctx"]

    def local(queries, prompt, cont, page_owner, lengths, offsets):
        own_prompt, own_cont = gather(prompt, cont, samples, ctx)
        base = (lax.axis_index("sample") * queries.shape[0]).reshape(1)
        return attend(queries, own_prompt, own_cont, page_owner, lengths, offsets, base)

    in_specs = (
        P("sample", None, "ctx"),
        P(None, "ctx", "sample"),
        P(None, "sample", "ctx", None),
        P(),
        P(),
        P(),
    )
    out_specs = P("sample", None, "ctx")
    return jax.shard_map(local, mesh=mesh, in_specs=in_specs, out_specs=out_specs, check_vma=False)
```

profile of v0, /device:TPU:0, one launch (start us, length us, event | category | flops | bytes accessed | tf_op | source)
XLA Modules:
  0.0 30.1 jit_solution(2431605651971164107)
XLA Ops:
  0.0 20.0 %gather_heads.1 = (bf16[2,8,2,32,128]{4,3,2,1,0:T(8,128)(2,1)}, bf16[2,2,8,2,32,128]{5,4,3,2,1,0:T(8,128)(2,1)}) custom-call(bf16[2,32,512]{2,1,0:T(8,128)(2,1)} %prompt_ref.1, bf16[2,2,32,1024]{3,2,1,0:T(8,128)(2,1)} %cont_ref.1), custom_call_target="tpu_custom_call" | custom-call | tf_op jit(solution)/shard_map/gather_heads/pallas_call | solution.py:251
  20.0 10.1 %attend.1 = bf16[2,512,512]{2,1,0:T(8,128)(2,1)} custom-call(s32[4]{0:T(128)} %lengths.1, s32[4]{0:T(128)} %offsets.1, s32[1]{0:T(128)} %bitcast.base, s32[1,512]{1,0:T(1,128)} %bitcast.6, bf16[2,512,512]{2,1,0:T(8,128)(2,1)} %q_ref.1, bf16[2,512,128]{2,1,0:T(8,128)(2,1)} %bitcast.5, bf16[2,2,512,128]{3,2,1,0:T(8,128)(2,1)} %bitcast.4), custom_call_target="tpu_custom_call" | custom-call | tf_op jit(solution)/shard_map/attend/pallas_call | solution.py:348
where the time goes:
time: 30.6 us; the launch traced here: 30.1 us
  Pallas kernels  30.1 us (98%)
    pallas_call x1, Pallas kernels, gather(): pl.pallas_call(functools.partial(gather_kernel, samples, ctx), out_shape=...  20 us
    pallas_call x1, Pallas kernels, attend(): pl.pallas_call(functools.partial(attend_kernel, block), out_shape=jax.Sha...  10.1 us

commit v1 on v0

--- a/solution.py
+++ b/solution.py
@@ -13,7 +13,8 @@
 MESH = pl.DeviceIdType.MESH
 
 neg_large = -1e30
-query_block = 128
+query_block = 256
+batches = 2
 
 
 def gather_kernel(
@@ -136,14 +137,22 @@
             copy.start()
             sends.append(copy)
 
-    def relay(buffer, index):
+    size = groups // batches
+
+    def batch(b):
+        return lax.rem(group // size + b, batches)
+
+    def batch_ref(kind, b, at):
+        return own_prompt.at[kind, pl.ds(batch(b) * size, size), at]
+
+    def relay(buffer, index, b):
         for k, sibling in enumerate(siblings):
             sends.append(
                 send(
                     buffer,
                     buffer,
-                    relay_send.at[index, k],
-                    relay_recv.at[index, rank],
+                    relay_send.at[index, b, k],
+                    relay_recv.at[index, batch(b), rank],
                     (sample, sibling),
                 )
             )
@@ -199,33 +208,47 @@
 
     if samples == 2:
         direct = lax.rem(group // shard_heads + sample, 2)
-        arrived = own_prompt.at[direct, :, rank]
-        crossed = own_prompt.at[1 - direct, :, rank]
-        for j in range(groups):
-            wait_slot(own_prompt.at[direct, j, rank], prompt_recv.at[j])
-        sends.append(send(arrived, arrived, cross_sems.at[0], cross_sems.at[1], (other, me)))
-        relay(arrived, 0)
+        for b in range(batches):
+            for j in range(size):
+                source = batch(b) * size + j
+                wait_slot(own_prompt.at[direct, source, rank], prompt_recv.at[source])
+            arrived = batch_ref(direct, b, rank)
+            sends.append(
+                send(
+                    arrived,
+                    arrived,
+                    cross_sems.at[0, b],
+                    cross_sems.at[1, batch(b)],
+                    (other, me),
+                )
+            )
+            relay(arrived, 0, b)
         for j in early:
             forward_cont(j)
-        wait_slot(crossed, cross_sems.at[1])
-        relay(crossed, 1)
+        for b in range(batches):
+            crossed = batch_ref(1 - direct, b, rank)
+            wait_slot(crossed, cross_sems.at[1, batch(b)])
+            relay(crossed, 1, b)
         for j in late:
             forward_cont(j)
         swap.wait_send()
     else:
         for j in range(groups):
             wait_slot(own_prompt.at[:, j, rank], prompt_recv.at[j])
-        relay(own_prompt.at[:, :, rank], 0)
+        for b in range(batches):
+            relay(own_prompt.at[:, pl.ds(batch(b) * size, size), rank], 0, b)
         for j in order:
             forward_cont(j)
 
     for k in range(1, copies):
         peer = lax.rem(rank + copies - k, copies)
-        if samples == 2:
-            wait_slot(own_prompt.at[direct, :, peer], relay_recv.at[0, peer])
-            wait_slot(own_prompt.at[1 - direct, :, peer], relay_recv.at[1, peer])
-        else:
-            wait_slot(own_prompt.at[:, :, peer], relay_recv.at[0, peer])
+        for b in range(batches):
+            rows = pl.ds(b * size, size)
+            if samples == 2:
+                wait_slot(own_prompt.at[direct, rows, peer], relay_recv.at[0, b, peer])
+                wait_slot(own_prompt.at[1 - direct, rows, peer], relay_recv.at[1, b, peer])
+            else:
+                wait_slot(own_prompt.at[:, rows, peer], relay_recv.at[0, b, peer])
         for j in range(groups):
             wait_slot(own_cont.at[:, :, j, peer], cont_recv.at[j * copies + peer])
 
@@ -259,9 +282,9 @@
         scratch_shapes=[
             pltpu.VMEM(prompt.shape[1:], prompt.dtype),
             pltpu.SemaphoreType.DMA((2,)),
-            pltpu.SemaphoreType.DMA((2,)),
-            pltpu.SemaphoreType.DMA((2, forwards)),
-            pltpu.SemaphoreType.DMA((2, copies)),
+            pltpu.SemaphoreType.DMA((2, batches)),
+            pltpu.SemaphoreType.DMA((2, batches, forwards)),
+            pltpu.SemaphoreType.DMA((2, batches, copies)),
             pltpu.SemaphoreType.DMA((2 * shard_heads * samples,)),
             pltpu.SemaphoreType.DMA((groups,)),
             pltpu.SemaphoreType.DMA((groups,)),
@@ -300,45 +323,52 @@
         @pl.when(live & (step == i))
         def _():
             extent = (i + 1) * block
-            q = jnp.concatenate(
-                [q_ref[0, :, h * HEAD_SIZE : (h + 1) * HEAD_SIZE] for h in range(heads)], axis=0
-            )
             owner = owner_ref[...]
             position = lax.broadcasted_iota(jnp.int32, (1, prompt_len), 1)
             seen = ((owner == 0) | (owner == sample + 1)) & (position < offsets[sample])
             bias = jnp.where(seen, 0.0, neg_large)
-            first = lax.dot_general(
-                q, prompt_ref[0], contract_last, preferred_element_type=jnp.float32
-            )
-            first = first + bias
-            second = lax.dot_general(
-                q, cont_ref[0, 0, :extent], contract_last, preferred_element_type=jnp.float32
-            )
             row = lax.broadcasted_iota(jnp.int32, (block, block), 0)
             col = lax.broadcasted_iota(jnp.int32, (block, block), 1)
             causal = jnp.where(col <= row, 0.0, neg_large)
-            causal = jnp.concatenate([causal] * heads, axis=0)
-            diagonal = second[:, i * block :] + causal
-            if i:
-                second = jnp.concatenate([second[:, : i * block], diagonal], axis=1)
-            else:
-                second = diagonal
-            row_max = jnp.maximum(
-                jnp.max(first, axis=1, keepdims=True), jnp.max(second, axis=1, keepdims=True)
-            )
-            first = jnp.exp2((first - row_max) * factor).astype(jnp.bfloat16)
-            second = jnp.exp2((second - row_max) * factor).astype(jnp.bfloat16)
-            total = jnp.dot(
-                first, with_ones(prompt_ref[1]), preferred_element_type=jnp.float32
-            ) + jnp.dot(
-                second, with_ones(cont_ref[1, 0, :extent]), preferred_element_type=jnp.float32
-            )
-            mixed = total[:, :HEAD_SIZE] / total[:, HEAD_SIZE:]
             place = i * block + lax.broadcasted_iota(jnp.int32, (block, HEAD_SIZE), 0)
+            prompt_values = with_ones(prompt_ref[1])
+            cont_values = with_ones(cont_ref[1, 0, :extent])
+
+            def scores(h):
+                q = q_ref[0, :, h * HEAD_SIZE : (h + 1) * HEAD_SIZE]
+                first = lax.dot_general(
+                    q, prompt_ref[0], contract_last, preferred_element_type=jnp.float32
+                )
+                second = lax.dot_general(
+                    q, cont_ref[0, 0, :extent], contract_last, preferred_element_type=jnp.float32
+                )
+                first = first + bias
+                diagonal = second[:, i * block :] + causal
+                if i:
+                    second = jnp.concatenate([second[:, : i * block], diagonal], axis=1)
+                else:
+                    second = diagonal
+                return first, second
+
+            def finish(h, first, second):
+                row_max = jnp.maximum(
+                    jnp.max(first, axis=1, keepdims=True), jnp.max(second, axis=1, keepdims=True)
+                )
+                first = jnp.exp2((first - row_max) * factor).astype(jnp.bfloat16)
+                second = jnp.exp2((second - row_max) * factor).astype(jnp.bfloat16)
+                total = jnp.dot(first, prompt_values, preferred_element_type=jnp.float32) + jnp.dot(
+                    second, cont_values, preferred_element_type=jnp.float32
+                )
+                mixed = total[:, :HEAD_SIZE] / total[:, HEAD_SIZE:]
+                out_ref[0, :, h * HEAD_SIZE : (h + 1) * HEAD_SIZE] = jnp.where(
+                    place < length, mixed, 0.0
+                ).astype(out_ref.dtype)
+
+            held = scores(0)
             for h in range(heads):
-                out_ref[0, :, h * HEAD_SIZE : (h + 1) * HEAD_SIZE] = jnp.where(
-                    place < length, mixed[h * block : (h + 1) * block], 0.0
-                ).astype(out_ref.dtype)
+                following = scores(h + 1) if h + 1 < heads else None
+                finish(h, *held)
+                held = following
 
 
 def attend(queries, own_prompt, own_cont, page_owner, lengths, offsets, base):

time: 30.6 us -> 27.7 us (0.905)
  Pallas kernels: 30.1 us -> 27.4 us
    pallas_call x1, Pallas kernels: 10.1 us -> 7.66 us  [attend(): pl.pallas_call(functools.partial(attend_kernel, block), out_shape=jax.Sha...]
    pallas_call x1, Pallas kernels: 20 us -> 19.7 us  [gather(): pl.pallas_call(functools.partial(gather_kernel, samples, ctx), out_shape=...]
where the time goes in v1:
time: 27.7 us; the launch traced here: 27.4 us
  Pallas kernels  27.4 us (99%)
    pallas_call x1, Pallas kernels, gather(): pl.pallas_call(functools.partial(gather_kernel, samples, ctx), out_shape=...  19.7 us
    pallas_call x1, Pallas kernels, attend(): pl.pallas_call(functools.partial(attend_kernel, block), out_shape=jax.Sha...  7.66 us

profile of v1, /device:TPU:0, one launch (start us, length us, event | category | flops | bytes accessed | tf_op | source)
XLA Modules:
  0.0 27.4 jit_solution(11815532176208158786)
XLA Ops:
  0.0 19.7 %gather_heads.1 = (bf16[2,8,2,32,128]{4,3,2,1,0:T(8,128)(2,1)}, bf16[2,2,8,2,32,128]{5,4,3,2,1,0:T(8,128)(2,1)}) custom-call(bf16[2,32,512]{2,1,0:T(8,128)(2,1)} %prompt_ref.1, bf16[2,2,32,1024]{3,2,1,0:T(8,128)(2,1)} %cont_ref.1), custom_call_target="tpu_custom_call" | custom-call | tf_op jit(solution)/shard_map/gather_heads/pallas_call | solution.py:274
  19.7 7.7 %attend.1 = bf16[2,512,512]{2,1,0:T(8,128)(2,1)} custom-call(s32[4]{0:T(128)} %lengths.1, s32[4]{0:T(128)} %offsets.1, s32[1]{0:T(128)} %bitcast.base, s32[1,512]{1,0:T(1,128)} %bitcast.6, bf16[2,512,512]{2,1,0:T(8,128)(2,1)} %q_ref.1, bf16[2,512,128]{2,1,0:T(8,128)(2,1)} %bitcast.5, bf16[2,2,512,128]{3,2,1,0:T(8,128)(2,1)} %bitcast.4), custom_call_target="tpu_custom_call" | custom-call | tf_op jit(solution)/shard_map/attend/pallas_call | solution.py:378
